TPU v7x, 32 devices: a whole 2x2x4 slice. The times are simulated.
32 devices in a mesh: row: 4 (over z), col: 2 (over x), rep: 4 (over y, core).
Axes of the slice: x: 2, y: 2, z: 4, core: 2. Of those that a mesh axis runs over, the one named last changes fastest.
Arguments:
- tensor_tiles: bfloat16 [64, 4, 128, 128], P(('row', 'col', 'rep')), may hold values from -12 to 12
- tile_pairs: int32 [64], P(('row', 'col', 'rep')), may hold values from 0 to 1, as said below
- tile_counts: int32 [32], P(('row', 'col', 'rep')), may hold values from 1 to 2, as said below
- occupied: bfloat16 [1024, 1024], P(('col', 'rep'), 'row'), as said below
- virtual: bfloat16 [1024, 1024], P(('col', 'rep'), 'row'), as said below
Outputs:
- polar: float32 [4, 4], replicated
- dressed: bfloat16 [1024, 4, 1024], P(('col', 'rep'), None, 'row')
Inputs may be any that keep to these rules, and one draw needn't show every extreme that they name: `tile_pairs`: the 2 entries of one block are distinct: a permutation of its tile pairs. `tile_counts`: some block has all 2 entries live. `occupied`: Symmetric. `virtual`: Symmetric.
All inputs are finite; a program needn't handle non-finite values.
Results may differ from a plain program's by a relative error of at most 0.0049.
Values may be sent and summed in bfloat16 or wider, within the bound.
No kernel may reach another device: no remote copies, remote signals or barrier semaphores. Data moves between devices by JAX's collectives and lax.ppermute only.
A program may use at most 128 MiB of HBM per device.

v0:
```python
import functools

import jax
import jax.numpy as jnp
from jax import lax
from jax.experimental import pallas as pl
from jax.experimental.pallas import tpu as pltpu
from jax.sharding import PartitionSpec as P

PLANE = ("col", "rep")
EVERY = ("row", "col", "rep")
VMEM = pl.BlockSpec(memory_space=pltpu.VMEM)
SMEM = pl.BlockSpec(memory_space=pltpu.SMEM)
ROOM = 48 << 20


def flip(value, axes, mask, count):
    return lax.ppermute(value, axes, [(i, i ^ mask) for i in range(count)])


def after(value, earlier):
    return lax.optimization_barrier((value, earlier))


def gather_row(value, n_row):
    found = {0: value}
    step = n_row // 2
    while step:
        found.update({k ^ step: flip(held, "row", step, n_row) for k, held in list(found.items())})
        step //= 2
    return [found[k] for k in range(n_row)]


def plane_index():
    return lax.axis_index("col") * lax.axis_size("rep") + lax.axis_index("rep")


def place_kernel(nu_tiles, counts_ref, pairs_any, tiles_any, weight_any, column_any, *refs):
    line_ref, bundle_ref, pairs_ref, tiles_ref, sems = refs
    slots, aux, tile, _ = tiles_ref.shape
    copies = [
        pltpu.make_async_copy(source, target, sems.at[i])
        for i, (source, target) in enumerate(
            [
                (tiles_any, tiles_ref),
                (pairs_any, pairs_ref),
                (weight_any, line_ref.at[aux]),
                (column_any, bundle_ref.at[aux]),
            ]
        )
    ]
    for copy in copies:
        copy.start()
    for copy in copies:
        copy.wait()
    for t in range(slots):
        pair = pairs_ref[t]
        rows = pl.ds(pl.multiple_of(pair // nu_tiles * tile, tile), tile)
        cols = pl.ds(pl.multiple_of(pair % nu_tiles * tile, tile), tile)

        @pl.when(t < counts_ref[0])
        def _():
            for out_ref in (line_ref, bundle_ref):
                out_ref[:aux, rows, cols] = tiles_ref[t]

        @pl.when(t >= counts_ref[0])
        def _():
            for out_ref in (line_ref, bundle_ref):
                out_ref[:aux, rows, cols] = jnp.zeros((aux, tile, tile), out_ref.dtype)


def place(tile_pairs, tile_counts, tensor_tiles, weight, column):
    slots, aux, tile, _ = tensor_tiles.shape
    mu, nu = weight.shape
    shape = jax.ShapeDtypeStruct((aux + 1, mu, nu), weight.dtype)
    stays = [pltpu.with_memory_space_constraint(value, pltpu.HBM) for value in (tile_pairs, tensor_tiles, weight, column)]
    return pl.pallas_call(
        functools.partial(place_kernel, nu // tile),
        out_shape=(shape, shape),
        in_specs=[SMEM] + [pl.BlockSpec(memory_space=pltpu.HBM)] * 4,
        out_specs=(VMEM, VMEM),
        scratch_shapes=[
            pltpu.SMEM(tile_pairs.shape, tile_pairs.dtype),
            pltpu.VMEM(tensor_tiles.shape, tensor_tiles.dtype),
            pltpu.SemaphoreType.DMA((4,)),
        ],
        compiler_params=pltpu.CompilerParams(vmem_limit_bytes=ROOM),
        cost_estimate=pl.CostEstimate(flops=0, bytes_accessed=6 * tensor_tiles.size, transcendentals=0),
        name="place",
    )(tile_counts, *stays)


def half_kernel(n_row, n_plane, *refs):
    lines, bundles = refs[:n_row], refs[n_row : n_row + n_plane]
    out_ref, panel = refs[n_row + n_plane :]
    planes, mu, nu = lines[0].shape
    aux = planes - 1
    row, plane = lax.axis_index("row"), plane_index()
    for k in range(n_plane):
        panel[pl.ds(pl.multiple_of((plane ^ k) * mu, mu), mu), :] = bundles[k][aux]
    for p in range(aux):
        total = jnp.zeros((mu, nu), jnp.float32)
        for k in range(n_row):
            at = pl.multiple_of((row ^ k) * nu, nu)
            total += jnp.dot(lines[k][p], panel[pl.ds(at, nu), :], preferred_element_type=jnp.float32)
        out_ref[:, p * nu : (p + 1) * nu] = total.astype(out_ref.dtype)


def half(lines, bundles):
    planes, mu, nu = lines[0].shape
    aux = planes - 1
    n_row, n_plane = len(lines), len(bundles)
    kind = lines[0].dtype
    return pl.pallas_call(
        functools.partial(half_kernel, n_row, n_plane),
        out_shape=jax.ShapeDtypeStruct((mu, aux * nu), kind),
        in_specs=[VMEM] * (n_row + n_plane),
        out_specs=VMEM,
        scratch_shapes=[pltpu.VMEM((n_plane * mu, nu), kind)],
        compiler_params=pltpu.CompilerParams(vmem_limit_bytes=ROOM),
        cost_estimate=pl.CostEstimate(
            flops=2 * aux * mu * nu * nu * n_row, bytes_accessed=4 * n_row * aux * mu * nu, transcendentals=0
        ),
        name="half_product",
    )(*lines, *bundles)


def share_kernel(n_row, n_plane, half_ref, *refs):
    weights, bundles = refs[:n_row], refs[n_row : n_row + n_plane]
    weight_ref, share_ref = refs[n_row + n_plane :]
    planes, mu, nu = weights[0].shape
    aux = planes - 1
    row, plane = lax.axis_index("row"), plane_index()
    rows = lax.broadcasted_iota(jnp.int32, share_ref.shape[1:], 0)
    lanes = lax.broadcasted_iota(jnp.int32, share_ref.shape[1:], 1)
    share = jnp.zeros(share_ref.shape[1:], jnp.float32)
    for k in range(n_row):
        weight_ref[:, pl.ds(pl.multiple_of((row ^ k) * nu, nu), nu)] = weights[k][weights[k].shape[0] - 1]
    for p in range(aux):
        mixed = jnp.zeros((mu, nu), jnp.float32)
        for k in range(n_plane):
            at = pl.multiple_of((plane ^ k) * mu, mu)
            mixed += jnp.dot(weight_ref[:, pl.ds(at, mu)], bundles[k][p], preferred_element_type=jnp.float32)
        for q in range(aux):
            product = mixed * half_ref[:, q * nu : (q + 1) * nu].astype(jnp.float32)
            folded = jnp.sum(product.reshape(mu // 8, 8, nu), axis=0)
            own = jnp.sum(jnp.sum(folded, axis=0, keepdims=True), axis=1, keepdims=True)
            share = jnp.where((rows == p) & (lanes == q), own, share)
    for i in range(n_row * n_plane):
        share_ref[i] = share


def share_of(half_block, weights, bundles):
    planes, mu, nu = weights[0].shape
    aux, n_row, n_plane = planes - 1, len(weights), len(bundles)
    return pl.pallas_call(
        functools.partial(share_kernel, n_row, n_plane),
        out_shape=(
            jax.ShapeDtypeStruct((mu, n_row * nu), weights[0].dtype),
            jax.ShapeDtypeStruct((n_row * n_plane, 8, 128), jnp.float32),
        ),
        in_specs=[VMEM] * (1 + n_row + n_plane),
        out_specs=(VMEM, VMEM),
        compiler_params=pltpu.CompilerParams(vmem_limit_bytes=ROOM),
        cost_estimate=pl.CostEstimate(
            flops=2 * aux * mu * mu * nu * n_plane, bytes_accessed=4 * n_plane * aux * mu * nu, transcendentals=0
        ),
        name="polar_share",
    )(half_block, *weights, *bundles)


def dress_kernel(n_plane, total_ao, weight_ref, *refs):
    halves, (shares_ref, out_ref, polar_ref) = refs[:n_plane], refs[n_plane:]
    mu, aux, nu = out_ref.shape
    plane = plane_index()
    for q in range(aux):
        total = jnp.zeros((mu, nu), jnp.float32)
        for k in range(n_plane):
            total += jnp.dot(
                weight_ref[:, pl.ds(pl.multiple_of((plane ^ k) * mu, mu), mu)],
                halves[k][:, q * nu : (q + 1) * nu],
                preferred_element_type=jnp.float32,
            )
        out_ref[:, q, :] = total.astype(out_ref.dtype)
    polar_ref[...] = jnp.sum(shares_ref[...], axis=0)[:aux, :aux] / total_ao


def dress(weight, halves, shares, aux, total_ao):
    mu, width = halves[0].shape
    n_plane = len(halves)
    return pl.pallas_call(
        functools.partial(dress_kernel, n_plane, total_ao),
        out_shape=(
            jax.ShapeDtypeStruct((mu, aux, width // aux), weight.dtype),
            jax.ShapeDtypeStruct((aux, aux), jnp.float32),
        ),
        in_specs=[VMEM] * (n_plane + 2),
        out_specs=(VMEM, VMEM),
        compiler_params=pltpu.CompilerParams(vmem_limit_bytes=ROOM),
        cost_estimate=pl.CostEstimate(
            flops=2 * mu * mu * width * n_plane, bytes_accessed=4 * n_plane * mu * width, transcendentals=0
        ),
        name="dress",
    )(weight, *halves, shares)


def on_device(tensor_tiles, tile_pairs, tile_counts, occupied, virtual):
    aux = tensor_tiles.shape[1]
    nu = virtual.shape[1]
    n_row, n_plane = lax.axis_size("row"), lax.axis_size("col") * lax.axis_size("rep")
    near = list(range(2, n_plane, 2))
    sibling = lambda value: flip(value, PLANE, 1, n_plane)

    line, bundle = place(tile_pairs, tile_counts, tensor_tiles, occupied, virtual)
    lines = gather_row(line, n_row)
    bundles = []
    for value in [bundle] + [flip(bundle, PLANE, k, n_plane) for k in near]:
        bundles += [value, sibling(value)]
    own = half(lines, bundles)

    arrivals = [flip(own, PLANE, k, n_plane) for k in near]
    other = sibling(own)
    weight, share = share_of(own, lines, bundles)
    shares, (other, arrivals) = after(lax.all_to_all(share, EVERY, 0, 0), (other, arrivals))
    halves = [own, other]
    for value in arrivals:
        halves += [value, sibling(value)]
    dressed, polar = dress(weight, halves, shares, aux, n_row * nu)
    return polar, dressed


def solution(mesh):
    return jax.shard_map(
        on_device,
        mesh=mesh,
        in_specs=(P(EVERY, None, None, None), P(EVERY), P(EVERY), P(PLANE, "row"), P(PLANE, "row")),
        out_specs=(P(), P(PLANE, None, "row")),
        check_vma=False,
    )
```

profile of v0, /device:TPU:0, one launch (start us, length us, event | category | flops | bytes accessed | tf_op | source)
XLA Modules:
  0.0 54.3 jit_solution(12559185202590592164)
XLA Ops:
  1.3 1.1 %place.1 = (bf16[5,128,256]{2,1,0:T(8,128)(2,1)S(1)}, bf16[5,128,256]{2,1,0:T(8,128)(2,1)S(1)}) custom-call(s32[1]{0:T(128)S(6)} %copy.7.counts_ref, s32[2]{0:T(128)} %pairs_any.1, bf16[2,4,128,128]{3,2,1,0:T(8,128)(2,1)} %tiles_any.1, bf16[128,256]{1,0:T(8,128)(2,1)} %weight_any.1, bf16[128,256]{1,0:T(8,128)(2,1)} %column_any.1), custom_call_target="tpu_custom_call" | custom-call | bytes 786432 | tf_op jit(solution)/shard_map/place/pallas_call | solution.py:77
  2.4 4.1 %collective-permute-start.1 = (bf16[5,128,256]{2,1,0:T(8,128)(2,1)S(1)}, bf16[5,128,256]{2,1,0:T(8,128)(2,1)S(1)}, u32[]{:S(2)}, u32[]{:S(2)}) collective-permute-start(bf16[5,128,256]{2,1,0:T(8,128)(2,1)S(1)} %get-tuple-element.13.refs_0_), channel_id=1, source_target_pairs={{0,16},{8,24},{16,0},{24,8},{1,17},{9,25},{17,1},{25,9},{2,18},{10... | collective-permute-start | bytes 983048 | tf_op jit(solution)/shard_map/ppermute | solution.py:18
  6.5 1.6 %collective-permute-start = (bf16[5,128,256]{2,1,0:T(8,128)(2,1)S(1)}, bf16[5,128,256]{2,1,0:T(8,128)(2,1)S(1)}, u32[]{:S(2)}, u32[]{:S(2)}) collective-permute-start(bf16[5,128,256]{2,1,0:T(8,128)(2,1)S(1)} %get-tuple-element.13.refs_0_), channel_id=1, source_target_pairs={{0,8},{8,0},{16,24},{24,16},{1,9},{9,1},{17,25},{25,17},{2,10},{10... | collective-permute-start | bytes 983048 | tf_op jit(solution)/shard_map/ppermute | solution.py:18
  8.1 2.4 %collective-permute-start.8 = (bf16[5,128,256]{2,1,0:T(8,128)(2,1)S(1)}, bf16[5,128,256]{2,1,0:T(8,128)(2,1)S(1)}, u32[]{:S(2)}, u32[]{:S(2)}) collective-permute-start(bf16[5,128,256]{2,1,0:T(8,128)(2,1)S(1)} %get-tuple-element.14.refs_4_), channel_id=1, source_target_pairs={{0,6},{1,7},{2,4},{3,5},{4,2},{5,3},{6,0},{7,1},{8,14},{9,15},{10,... | collective-permute-start | bytes 983048 | tf_op jit(solution)/shard_map/ppermute | solution.py:18
  10.5 0.5 collective-permute-start.6
  11.1 0.5 collective-permute-start.4
  11.6 9.8 %collective-permute-done.1.refs_2_ = bf16[5,128,256]{2,1,0:T(8,128)(2,1)S(1)} collective-permute-done((bf16[5,128,256]{2,1,0:T(8,128)(2,1)S(1)}, bf16[5,128,256]{2,1,0:T(8,128)(2,1)S(1)}, u32[]{:S(2)}, u32[]{:S(2)}) %collective-permute-start.1) | collective-permute-done | bytes 327712 | tf_op jit(solution)/shard_map/ppermute | solution.py:18
  21.5 1.5 %collective-permute-start.2 = (bf16[5,128,256]{2,1,0:T(8,128)(2,1)S(1)}, bf16[5,128,256]{2,1,0:T(8,128)(2,1)S(1)}, u32[]{:S(2)}, u32[]{:S(2)}) collective-permute-start(bf16[5,128,256]{2,1,0:T(8,128)(2,1)S(1)} %collective-permute-done.1.refs_2_), channel_id=1, source_target_pairs={{0,8},{8,0},{16,24},{24,16},{1,9},{9,1},{17,25},{25,17},{2,10},{10... | collective-permute-start | bytes 983048 | tf_op jit(solution)/shard_map/ppermute | solution.py:18
  23.0 2.0 %collective-permute-done.6.refs_8_ = bf16[5,128,256]{2,1,0:T(8,128)(2,1)S(1)} collective-permute-done((bf16[5,128,256]{2,1,0:T(8,128)(2,1)S(1)}, bf16[5,128,256]{2,1,0:T(8,128)(2,1)S(1)}, u32[]{:S(2)}, u32[]{:S(2)}) %collective-permute-start.6) | collective-permute-done | bytes 327712 | tf_op jit(solution)/shard_map/ppermute | solution.py:18
  25.0 0.5 collective-permute-start.5
  25.5 6.0 %collective-permute-done.2.refs_3_ = bf16[5,128,256]{2,1,0:T(8,128)(2,1)S(1)} collective-permute-done((bf16[5,128,256]{2,1,0:T(8,128)(2,1)S(1)}, bf16[5,128,256]{2,1,0:T(8,128)(2,1)S(1)}, u32[]{:S(2)}, u32[]{:S(2)}) %collective-permute-start.2) | collective-permute-done | bytes 327712 | tf_op jit(solution)/shard_map/ppermute | solution.py:18
  31.5 0.5 half_product.1.half_ref.refs_0_
  32.0 2.6 %collective-permute-start.13 = (bf16[128,1024]{1,0:T(8,128)(2,1)S(1)}, bf16[128,1024]{1,0:T(8,128)(2,1)S(1)}, u32[]{:S(2)}, u32[]{:S(2)}) collective-permute-start(bf16[128,1024]{1,0:T(8,128)(2,1)S(1)} %half_product.1.half_ref.refs_0_), channel_id=1, source_target_pairs={{0,6},{1,7},{2,4},{3,5},{4,2},{5,3},{6,0},{7,1},{8,14},{9,15},{10,... | collective-permute-start | bytes 786440 | tf_op jit(solution)/shard_map/ppermute | solution.py:18
  34.5 0.5 collective-permute-start.12
  35.1 0.5 collective-permute-start.11
  35.5 0.9 %polar_share.1 = (bf16[128,1024]{1,0:T(8,128)(2,1)S(1)}, f32[32,8,128]{2,1,0:T(8,128)S(1)}) custom-call(bf16[128,1024]{1,0:T(8,128)(2,1)S(1)} %half_product.1.half_ref.refs_0_, bf16[5,128,256]{2,1,0:T(8,128)(2,1)S(1)} %get-tuple-element.13.refs_0_, bf16[5,128,256]{2,1,0:T(8,128)(2,1)S(1)} %collective-permute-done.refs_1_, ...), custom_call_target="tpu_custom_call" | custom-call | flops 268435456 | bytes 4194304 | tf_op jit(solution)/shard_map/polar_share/pallas_call | solution.py:156
  36.4 13.8 %all_to_all.5.refs_8_ = f32[32,8,128]{2,1,0:T(8,128)S(1)} all-to-all(f32[32,8,128]{2,1,0:T(8,128)S(1)} %get-tuple-element.16), channel_id=1, replica_groups=mesh['row'=4,'col'=2,'rep'=4] {'row','col','rep'}, dimensions={0} | all-to-all | bytes 262144 | tf_op jit(solution)/shard_map/all_to_all | solution.py:224
  50.2 0.3 collective-permute-start.14
  50.5 0.3 collective-permute-start.15
  50.8 0.2 collective-permute-start.16
  51.0 0.8 %collective-permute-done.14.refs_3_ = bf16[128,1024]{1,0:T(8,128)(2,1)S(1)} collective-permute-done((bf16[128,1024]{1,0:T(8,128)(2,1)S(1)}, bf16[128,1024]{1,0:T(8,128)(2,1)S(1)}, u32[]{:S(2)}, u32[]{:S(2)}) %collective-permute-start.14) | collective-permute-done | bytes 262176 | tf_op jit(solution)/shard_map/ppermute | solution.py:18
  51.8 0.4 collective-permute-done.15.refs_5_
  52.2 0.4 collective-permute-done.16.refs_7_
  52.6 1.7 %dress.1 = (bf16[128,4,256]{2,1,0:T(4,128)(2,1)}, f32[4,4]{1,0:T(4,128)}) custom-call(bf16[128,1024]{1,0:T(8,128)(2,1)S(1)} %get-tuple-element.15.weight_ref, bf16[128,1024]{1,0:T(8,128)(2,1)S(1)} %half_product.1.half_ref.refs_0_, bf16[128,1024]{1,0:T(8,128)(2,1)S(1)} %collective-permute-done.10.refs_1_, ...), custom_call_target="tpu_custom_call" | custom-call | flops 268435456 | bytes 4194304 | tf_op jit(solution)/shard_map/dress/pallas_call | solution.py:191
  (15 shorter events, 0.2 us)
Async XLA Ops:
  2.4 18.9 %collective-permute-start.1 = (bf16[5,128,256]{2,1,0:T(8,128)(2,1)S(1)}, bf16[5,128,256]{2,1,0:T(8,128)(2,1)S(1)}, u32[]{:S(2)}, u32[]{:S(2)}) collective-permute-start(bf16[5,128,256]{2,1,0:T(8,128)(2,1)S(1)} %get-tuple-element.13.refs_0_), channel_id=1, source_target_pairs={{0,16},{8,24},{16,0},{24,8},{1,17},{9,25},{17,1},{25,9},{2,18},{10... | collective-permute-start | bytes 983048 | tf_op jit(solution)/shard_map/ppermute | solution.py:18
  6.5 15.0 %collective-permute-start = (bf16[5,128,256]{2,1,0:T(8,128)(2,1)S(1)}, bf16[5,128,256]{2,1,0:T(8,128)(2,1)S(1)}, u32[]{:S(2)}, u32[]{:S(2)}) collective-permute-start(bf16[5,128,256]{2,1,0:T(8,128)(2,1)S(1)} %get-tuple-element.13.refs_0_), channel_id=1, source_target_pairs={{0,8},{8,0},{16,24},{24,16},{1,9},{9,1},{17,25},{25,17},{2,10},{10... | collective-permute-start | bytes 983048 | tf_op jit(solution)/shard_map/ppermute | solution.py:18
  8.1 14.9 %collective-permute-start.8 = (bf16[5,128,256]{2,1,0:T(8,128)(2,1)S(1)}, bf16[5,128,256]{2,1,0:T(8,128)(2,1)S(1)}, u32[]{:S(2)}, u32[]{:S(2)}) collective-permute-start(bf16[5,128,256]{2,1,0:T(8,128)(2,1)S(1)} %get-tuple-element.14.refs_4_), channel_id=1, source_target_pairs={{0,6},{1,7},{2,4},{3,5},{4,2},{5,3},{6,0},{7,1},{8,14},{9,15},{10,... | collective-permute-start | bytes 983048 | tf_op jit(solution)/shard_map/ppermute | solution.py:18
  10.5 14.5 %collective-permute-start.6 = (bf16[5,128,256]{2,1,0:T(8,128)(2,1)S(1)}, bf16[5,128,256]{2,1,0:T(8,128)(2,1)S(1)}, u32[]{:S(2)}, u32[]{:S(2)}) collective-permute-start(bf16[5,128,256]{2,1,0:T(8,128)(2,1)S(1)} %get-tuple-element.14.refs_4_), channel_id=1, source_target_pairs={{0,4},{1,5},{2,6},{3,7},{4,0},{5,1},{6,2},{7,3},{8,12},{9,13},{10,... | collective-permute-start | bytes 983048 | tf_op jit(solution)/shard_map/ppermute | solution.py:18
  11.1 13.9 %collective-permute-start.4 = (bf16[5,128,256]{2,1,0:T(8,128)(2,1)S(1)}, bf16[5,128,256]{2,1,0:T(8,128)(2,1)S(1)}, u32[]{:S(2)}, u32[]{:S(2)}) collective-permute-start(bf16[5,128,256]{2,1,0:T(8,128)(2,1)S(1)} %get-tuple-element.14.refs_4_), channel_id=1, source_target_pairs={{0,2},{1,3},{2,0},{3,1},{4,6},{5,7},{6,4},{7,5},{8,10},{9,11},{10,... | collective-permute-start | bytes 983048 | tf_op jit(solution)/shard_map/ppermute | solution.py:18
  21.3 4.2 %collective-permute-start.3 = (bf16[5,128,256]{2,1,0:T(8,128)(2,1)S(1)}, bf16[5,128,256]{2,1,0:T(8,128)(2,1)S(1)}, u32[]{:S(2)}, u32[]{:S(2)}) collective-permute-start(bf16[5,128,256]{2,1,0:T(8,128)(2,1)S(1)} %get-tuple-element.14.refs_4_), channel_id=1, source_target_pairs={{0,1},{1,0},{2,3},{3,2},{4,5},{5,4},{6,7},{7,6},{8,9},{9,8},{10,11... | collective-permute-start | bytes 983048 | tf_op jit(solution)/shard_map/ppermute | solution.py:18
  21.5 9.9 %collective-permute-start.2 = (bf16[5,128,256]{2,1,0:T(8,128)(2,1)S(1)}, bf16[5,128,256]{2,1,0:T(8,128)(2,1)S(1)}, u32[]{:S(2)}, u32[]{:S(2)}) collective-permute-start(bf16[5,128,256]{2,1,0:T(8,128)(2,1)S(1)} %collective-permute-done.1.refs_2_), channel_id=1, source_target_pairs={{0,8},{8,0},{16,24},{24,16},{1,9},{9,1},{17,25},{25,17},{2,10},{10... | collective-permute-start | bytes 983048 | tf_op jit(solution)/shard_map/ppermute | solution.py:18
  23.0 8.5 %collective-permute-start.9 = (bf16[5,128,256]{2,1,0:T(8,128)(2,1)S(1)}, bf16[5,128,256]{2,1,0:T(8,128)(2,1)S(1)}, u32[]{:S(2)}, u32[]{:S(2)}) collective-permute-start(bf16[5,128,256]{2,1,0:T(8,128)(2,1)S(1)} %collective-permute-done.8.refs_10_), channel_id=1, source_target_pairs={{0,1},{1,0},{2,3},{3,2},{4,5},{5,4},{6,7},{7,6},{8,9},{9,8},{10,11... | collective-permute-start | bytes 983048 | tf_op jit(solution)/shard_map/ppermute | solution.py:18
  25.0 6.5 %collective-permute-start.7 = (bf16[5,128,256]{2,1,0:T(8,128)(2,1)S(1)}, bf16[5,128,256]{2,1,0:T(8,128)(2,1)S(1)}, u32[]{:S(2)}, u32[]{:S(2)}) collective-permute-start(bf16[5,128,256]{2,1,0:T(8,128)(2,1)S(1)} %collective-permute-done.6.refs_8_), channel_id=1, source_target_pairs={{0,1},{1,0},{2,3},{3,2},{4,5},{5,4},{6,7},{7,6},{8,9},{9,8},{10,11... | collective-permute-start | bytes 983048 | tf_op jit(solution)/shard_map/ppermute | solution.py:18
  25.0 6.5 %collective-permute-start.5 = (bf16[5,128,256]{2,1,0:T(8,128)(2,1)S(1)}, bf16[5,128,256]{2,1,0:T(8,128)(2,1)S(1)}, u32[]{:S(2)}, u32[]{:S(2)}) collective-permute-start(bf16[5,128,256]{2,1,0:T(8,128)(2,1)S(1)} %collective-permute-done.4.refs_6_), channel_id=1, source_target_pairs={{0,1},{1,0},{2,3},{3,2},{4,5},{5,4},{6,7},{7,6},{8,9},{9,8},{10,11... | collective-permute-start | bytes 983048 | tf_op jit(solution)/shard_map/ppermute | solution.py:18
  32.0 18.2 %collective-permute-start.13 = (bf16[128,1024]{1,0:T(8,128)(2,1)S(1)}, bf16[128,1024]{1,0:T(8,128)(2,1)S(1)}, u32[]{:S(2)}, u32[]{:S(2)}) collective-permute-start(bf16[128,1024]{1,0:T(8,128)(2,1)S(1)} %half_product.1.half_ref.refs_0_), channel_id=1, source_target_pairs={{0,6},{1,7},{2,4},{3,5},{4,2},{5,3},{6,0},{7,1},{8,14},{9,15},{10,... | collective-permute-start | bytes 786440 | tf_op jit(solution)/shard_map/ppermute | solution.py:18
  34.5 15.7 %collective-permute-start.12 = (bf16[128,1024]{1,0:T(8,128)(2,1)S(1)}, bf16[128,1024]{1,0:T(8,128)(2,1)S(1)}, u32[]{:S(2)}, u32[]{:S(2)}) collective-permute-start(bf16[128,1024]{1,0:T(8,128)(2,1)S(1)} %half_product.1.half_ref.refs_0_), channel_id=1, source_target_pairs={{0,4},{1,5},{2,6},{3,7},{4,0},{5,1},{6,2},{7,3},{8,12},{9,13},{10,... | collective-permute-start | bytes 786440 | tf_op jit(solution)/shard_map/ppermute | solution.py:18
  35.1 15.2 %collective-permute-start.11 = (bf16[128,1024]{1,0:T(8,128)(2,1)S(1)}, bf16[128,1024]{1,0:T(8,128)(2,1)S(1)}, u32[]{:S(2)}, u32[]{:S(2)}) collective-permute-start(bf16[128,1024]{1,0:T(8,128)(2,1)S(1)} %half_product.1.half_ref.refs_0_), channel_id=1, source_target_pairs={{0,2},{1,3},{2,0},{3,1},{4,6},{5,7},{6,4},{7,5},{8,10},{9,11},{10,... | collective-permute-start | bytes 786440 | tf_op jit(solution)/shard_map/ppermute | solution.py:18
  35.5 14.7 %collective-permute-start.10 = (bf16[128,1024]{1,0:T(8,128)(2,1)S(1)}, bf16[128,1024]{1,0:T(8,128)(2,1)S(1)}, u32[]{:S(2)}, u32[]{:S(2)}) collective-permute-start(bf16[128,1024]{1,0:T(8,128)(2,1)S(1)} %half_product.1.half_ref.refs_0_), channel_id=1, source_target_pairs={{0,1},{1,0},{2,3},{3,2},{4,5},{5,4},{6,7},{7,6},{8,9},{9,8},{10,11... | collective-permute-start | bytes 786440 | tf_op jit(solution)/shard_map/ppermute | solution.py:18
  50.2 1.6 %collective-permute-start.14 = (bf16[128,1024]{1,0:T(8,128)(2,1)S(1)}, bf16[128,1024]{1,0:T(8,128)(2,1)S(1)}, u32[]{:S(2)}, u32[]{:S(2)}) collective-permute-start(bf16[128,1024]{1,0:T(8,128)(2,1)S(1)} %collective-permute-done.11.refs_2_), channel_id=1, source_target_pairs={{0,1},{1,0},{2,3},{3,2},{4,5},{5,4},{6,7},{7,6},{8,9},{9,8},{10,11... | collective-permute-start | bytes 786440 | tf_op jit(solution)/shard_map/ppermute | solution.py:18
  50.5 1.7 %collective-permute-start.15 = (bf16[128,1024]{1,0:T(8,128)(2,1)S(1)}, bf16[128,1024]{1,0:T(8,128)(2,1)S(1)}, u32[]{:S(2)}, u32[]{:S(2)}) collective-permute-start(bf16[128,1024]{1,0:T(8,128)(2,1)S(1)} %collective-permute-done.12.refs_4_), channel_id=1, source_target_pairs={{0,1},{1,0},{2,3},{3,2},{4,5},{5,4},{6,7},{7,6},{8,9},{9,8},{10,11... | collective-permute-start | bytes 786440 | tf_op jit(solution)/shard_map/ppermute | solution.py:18
  50.8 1.8 %collective-permute-start.16 = (bf16[128,1024]{1,0:T(8,128)(2,1)S(1)}, bf16[128,1024]{1,0:T(8,128)(2,1)S(1)}, u32[]{:S(2)}, u32[]{:S(2)}) collective-permute-start(bf16[128,1024]{1,0:T(8,128)(2,1)S(1)} %collective-permute-done.13.refs_6_), channel_id=1, source_target_pairs={{0,1},{1,0},{2,3},{3,2},{4,5},{5,4},{6,7},{7,6},{8,9},{9,8},{10,11... | collective-permute-start | bytes 786440 | tf_op jit(solution)/shard_map/ppermute | solution.py:18
where the time goes:
time: 54.5 us; the launch traced here: 54.3 us
  waiting for transfers between devices  19.5 us (36%)
  starting transfers between devices  15.5 us (28%)
  blocking collectives  13.8 us (25%)
  Pallas kernels  4.19 us (8%)
  between operations  1.33 us (2%)
    ppermute x17, waiting for transfers between devices, flip(): return lax.ppermute(value, axes, [(i, i ^ mask) for i in range(count)])  19.5 us
    ppermute x17, starting transfers between devices, flip(): return lax.ppermute(value, axes, [(i, i ^ mask) for i in range(count)])  15.5 us
    all_to_all x1, blocking collectives, on_device(): lax.all_to_all(share, EVERY, 0, 0)  13.8 us
    pallas_call x1, Pallas kernels, dress(): pl.pallas_call(functools.partial(dress_kernel, n_plane, total_ao), out_sh...  1.74 us
    pallas_call x1, Pallas kernels, place(): pl.pallas_call(functools.partial(place_kernel, nu // tile), out_shape=(sh...  1.1 us
  transfers between devices with their start and end apart: 17, of which 7 were waited for; matrix products, arithmetic and copies ran while one was open for 0% of the time, Pallas kernels for 2%

commit v1 on v0

--- a/solution.py
+++ b/solution.py
@@ -131,7 +131,6 @@
     planes, mu, nu = weights[0].shape
     aux = planes - 1
     row, plane = lax.axis_index("row"), plane_index()
-    rows = lax.broadcasted_iota(jnp.int32, share_ref.shape[1:], 0)
     lanes = lax.broadcasted_iota(jnp.int32, share_ref.shape[1:], 1)
     share = jnp.zeros(share_ref.shape[1:], jnp.float32)
     for k in range(n_row):
@@ -145,7 +144,7 @@
             product = mixed * half_ref[:, q * nu : (q + 1) * nu].astype(jnp.float32)
             folded = jnp.sum(product.reshape(mu // 8, 8, nu), axis=0)
             own = jnp.sum(jnp.sum(folded, axis=0, keepdims=True), axis=1, keepdims=True)
-            share = jnp.where((rows == p) & (lanes == q), own, share)
+            share = jnp.where(lanes == p * aux + q, own, share)
     for i in range(n_row * n_plane):
         share_ref[i] = share
 
@@ -157,7 +156,7 @@
         functools.partial(share_kernel, n_row, n_plane),
         out_shape=(
             jax.ShapeDtypeStruct((mu, n_row * nu), weights[0].dtype),
-            jax.ShapeDtypeStruct((n_row * n_plane, 8, 128), jnp.float32),
+            jax.ShapeDtypeStruct((n_row * n_plane, 1, 128), jnp.float32),
         ),
         in_specs=[VMEM] * (1 + n_row + n_plane),
         out_specs=(VMEM, VMEM),
@@ -173,6 +172,7 @@
     halves, (shares_ref, out_ref, polar_ref) = refs[:n_plane], refs[n_plane:]
     mu, aux, nu = out_ref.shape
     plane = plane_index()
+    sums = []
     for q in range(aux):
         total = jnp.zeros((mu, nu), jnp.float32)
         for k in range(n_plane):
@@ -181,8 +181,11 @@
                 halves[k][:, q * nu : (q + 1) * nu],
                 preferred_element_type=jnp.float32,
             )
-        out_ref[:, q, :] = total.astype(out_ref.dtype)
-    polar_ref[...] = jnp.sum(shares_ref[...], axis=0)[:aux, :aux] / total_ao
+        sums.append(total)
+    out_ref[...] = jnp.stack(sums, axis=1).astype(out_ref.dtype)
+    polar = jnp.sum(shares_ref[...], axis=0) / total_ao
+    for p in range(aux):
+        polar_ref[p : p + 1, :] = polar[:, p * aux : (p + 1) * aux]
 
 
 def dress(weight, halves, shares, aux, total_ao):

time: 54.5 us -> 53.5 us (0.982)
  blocking collectives: 13.8 us -> 12.7 us
    all_to_all x1, blocking collectives: 13.8 us -> 12.7 us  [on_device(): lax.all_to_all(share, EVERY, 0, 0)]
where the time goes in v1:
time: 53.5 us; the launch traced here: 53.3 us
  waiting for transfers between devices  19.6 us (37%)
  starting transfers between devices  15.4 us (29%)
  blocking collectives  12.7 us (24%)
  Pallas kernels  4.24 us (8%)
  between operations  1.34 us (3%)
    ppermute x17, waiting for transfers between devices, flip(): return lax.ppermute(value, axes, [(i, i ^ mask) for i in range(count)])  19.6 us
    ppermute x17, starting transfers between devices, flip(): return lax.ppermute(value, axes, [(i, i ^ mask) for i in range(count)])  15.4 us
    all_to_all x1, blocking collectives, on_device(): lax.all_to_all(share, EVERY, 0, 0)  12.7 us
    pallas_call x1, Pallas kernels, dress(): pl.pallas_call(functools.partial(dress_kernel, n_plane, total_ao), out_sh...  1.79 us
    pallas_call x1, Pallas kernels, place(): pl.pallas_call(functools.partial(place_kernel, nu // tile), out_shape=(sh...  1.1 us
  transfers between devices with their start and end apart: 17, of which 7 were waited for; matrix products, arithmetic and copies ran while one was open for 0% of the time, Pallas kernels for 2%

profile of v1, /device:TPU:0, one launch (start us, length us, event | category | flops | bytes accessed | tf_op | source)
XLA Modules:
  0.0 53.3 jit_solution(18052666631066230176)
XLA Ops:
  1.3 1.1 %place.1 = (bf16[5,128,256]{2,1,0:T(8,128)(2,1)S(1)}, bf16[5,128,256]{2,1,0:T(8,128)(2,1)S(1)}) custom-call(s32[1]{0:T(128)S(6)} %copy.7.counts_ref, s32[2]{0:T(128)} %pairs_any.1, bf16[2,4,128,128]{3,2,1,0:T(8,128)(2,1)} %tiles_any.1, bf16[128,256]{1,0:T(8,128)(2,1)} %weight_any.1, bf16[128,256]{1,0:T(8,128)(2,1)} %column_any.1), custom_call_target="tpu_custom_call" | custom-call | bytes 786432 | tf_op jit(solution)/shard_map/place/pallas_call | solution.py:77
  2.4 4.1 %collective-permute-start.1 = (bf16[5,128,256]{2,1,0:T(8,128)(2,1)S(1)}, bf16[5,128,256]{2,1,0:T(8,128)(2,1)S(1)}, u32[]{:S(2)}, u32[]{:S(2)}) collective-permute-start(bf16[5,128,256]{2,1,0:T(8,128)(2,1)S(1)} %get-tuple-element.13.refs_0_), channel_id=1, source_target_pairs={{0,16},{8,24},{16,0},{24,8},{1,17},{9,25},{17,1},{25,9},{2,18},{10... | collective-permute-start | bytes 983048 | tf_op jit(solution)/shard_map/ppermute | solution.py:18
  6.5 1.6 %collective-permute-start = (bf16[5,128,256]{2,1,0:T(8,128)(2,1)S(1)}, bf16[5,128,256]{2,1,0:T(8,128)(2,1)S(1)}, u32[]{:S(2)}, u32[]{:S(2)}) collective-permute-start(bf16[5,128,256]{2,1,0:T(8,128)(2,1)S(1)} %get-tuple-element.13.refs_0_), channel_id=1, source_target_pairs={{0,8},{8,0},{16,24},{24,16},{1,9},{9,1},{17,25},{25,17},{2,10},{10... | collective-permute-start | bytes 983048 | tf_op jit(solution)/shard_map/ppermute | solution.py:18
  8.1 2.4 %collective-permute-start.8 = (bf16[5,128,256]{2,1,0:T(8,128)(2,1)S(1)}, bf16[5,128,256]{2,1,0:T(8,128)(2,1)S(1)}, u32[]{:S(2)}, u32[]{:S(2)}) collective-permute-start(bf16[5,128,256]{2,1,0:T(8,128)(2,1)S(1)} %get-tuple-element.14.refs_4_), channel_id=1, source_target_pairs={{0,6},{1,7},{2,4},{3,5},{4,2},{5,3},{6,0},{7,1},{8,14},{9,15},{10,... | collective-permute-start | bytes 983048 | tf_op jit(solution)/shard_map/ppermute | solution.py:18
  10.5 0.5 %collective-permute-start.6 = (bf16[5,128,256]{2,1,0:T(8,128)(2,1)S(1)}, bf16[5,128,256]{2,1,0:T(8,128)(2,1)S(1)}, u32[]{:S(2)}, u32[]{:S(2)}) collective-permute-start(bf16[5,128,256]{2,1,0:T(8,128)(2,1)S(1)} %get-tuple-element.14.refs_4_), channel_id=1, source_target_pairs={{0,4},{1,5},{2,6},{3,7},{4,0},{5,1},{6,2},{7,3},{8,12},{9,13},{10,... | collective-permute-start | bytes 983048 | tf_op jit(solution)/shard_map/ppermute | solution.py:18
  11.0 0.5 collective-permute-start.4
  11.6 9.8 %collective-permute-done.1.refs_2_ = bf16[5,128,256]{2,1,0:T(8,128)(2,1)S(1)} collective-permute-done((bf16[5,128,256]{2,1,0:T(8,128)(2,1)S(1)}, bf16[5,128,256]{2,1,0:T(8,128)(2,1)S(1)}, u32[]{:S(2)}, u32[]{:S(2)}) %collective-permute-start.1) | collective-permute-done | bytes 327712 | tf_op jit(solution)/shard_map/ppermute | solution.py:18
  21.3 0.2 collective-permute-done.refs_1_
  21.5 1.5 %collective-permute-start.2 = (bf16[5,128,256]{2,1,0:T(8,128)(2,1)S(1)}, bf16[5,128,256]{2,1,0:T(8,128)(2,1)S(1)}, u32[]{:S(2)}, u32[]{:S(2)}) collective-permute-start(bf16[5,128,256]{2,1,0:T(8,128)(2,1)S(1)} %collective-permute-done.1.refs_2_), channel_id=1, source_target_pairs={{0,8},{8,0},{16,24},{24,16},{1,9},{9,1},{17,25},{25,17},{2,10},{10... | collective-permute-start | bytes 983048 | tf_op jit(solution)/shard_map/ppermute | solution.py:18
  23.0 2.0 %collective-permute-done.6.refs_8_ = bf16[5,128,256]{2,1,0:T(8,128)(2,1)S(1)} collective-permute-done((bf16[5,128,256]{2,1,0:T(8,128)(2,1)S(1)}, bf16[5,128,256]{2,1,0:T(8,128)(2,1)S(1)}, u32[]{:S(2)}, u32[]{:S(2)}) %collective-permute-start.6) | collective-permute-done | bytes 327712 | tf_op jit(solution)/shard_map/ppermute | solution.py:18
  25.0 0.5 collective-permute-start.5
  25.5 6.0 %collective-permute-done.2.refs_3_ = bf16[5,128,256]{2,1,0:T(8,128)(2,1)S(1)} collective-permute-done((bf16[5,128,256]{2,1,0:T(8,128)(2,1)S(1)}, bf16[5,128,256]{2,1,0:T(8,128)(2,1)S(1)}, u32[]{:S(2)}, u32[]{:S(2)}) %collective-permute-start.2) | collective-permute-done | bytes 327712 | tf_op jit(solution)/shard_map/ppermute | solution.py:18
  31.5 0.5 half_product.1.half_ref.refs_0_
  32.0 2.6 %collective-permute-start.13 = (bf16[128,1024]{1,0:T(8,128)(2,1)S(1)}, bf16[128,1024]{1,0:T(8,128)(2,1)S(1)}, u32[]{:S(2)}, u32[]{:S(2)}) collective-permute-start(bf16[128,1024]{1,0:T(8,128)(2,1)S(1)} %half_product.1.half_ref.refs_0_), channel_id=1, source_target_pairs={{0,6},{1,7},{2,4},{3,5},{4,2},{5,3},{6,0},{7,1},{8,14},{9,15},{10,... | collective-permute-start | bytes 786440 | tf_op jit(solution)/shard_map/ppermute | solution.py:18
  34.5 0.5 %collective-permute-start.12 = (bf16[128,1024]{1,0:T(8,128)(2,1)S(1)}, bf16[128,1024]{1,0:T(8,128)(2,1)S(1)}, u32[]{:S(2)}, u32[]{:S(2)}) collective-permute-start(bf16[128,1024]{1,0:T(8,128)(2,1)S(1)} %half_product.1.half_ref.refs_0_), channel_id=1, source_target_pairs={{0,4},{1,5},{2,6},{3,7},{4,0},{5,1},{6,2},{7,3},{8,12},{9,13},{10,... | collective-permute-start | bytes 786440 | tf_op jit(solution)/shard_map/ppermute | solution.py:18
  35.1 0.5 collective-permute-start.11
  35.5 0.9 %polar_share.1 = (bf16[128,1024]{1,0:T(8,128)(2,1)S(1)}, f32[32,1,128]{2,1,0:T(1,128)S(1)}) custom-call(bf16[128,1024]{1,0:T(8,128)(2,1)S(1)} %half_product.1.half_ref.refs_0_, bf16[5,128,256]{2,1,0:T(8,128)(2,1)S(1)} %get-tuple-element.13.refs_0_, bf16[5,128,256]{2,1,0:T(8,128)(2,1)S(1)} %collective-permute-done.refs_1_, ...), custom_call_target="tpu_custom_call" | custom-call | flops 268435456 | bytes 4194304 | tf_op jit(solution)/shard_map/polar_share/pallas_call | solution.py:155
  36.4 12.7 %all_to_all.5.refs_8_ = f32[32,1,128]{2,1,0:T(1,128)S(1)} all-to-all(f32[32,1,128]{2,1,0:T(1,128)S(1)} %get-tuple-element.16), channel_id=1, replica_groups=mesh['row'=4,'col'=2,'rep'=4] {'row','col','rep'}, dimensions={0} | all-to-all | bytes 32768 | tf_op jit(solution)/shard_map/all_to_all | solution.py:227
  49.2 0.5 collective-permute-start.15
  49.7 0.1 collective-permute-start.16
  49.8 0.9 %collective-permute-done.14.refs_3_ = bf16[128,1024]{1,0:T(8,128)(2,1)S(1)} collective-permute-done((bf16[128,1024]{1,0:T(8,128)(2,1)S(1)}, bf16[128,1024]{1,0:T(8,128)(2,1)S(1)}, u32[]{:S(2)}, u32[]{:S(2)}) %collective-permute-start.14) | collective-permute-done | bytes 262176 | tf_op jit(solution)/shard_map/ppermute | solution.py:18
  50.8 0.4 collective-permute-done.15.refs_5_
  51.1 0.4 collective-permute-done.16.refs_7_
  51.5 1.8 %dress.1 = (bf16[128,4,256]{2,1,0:T(4,128)(2,1)}, f32[4,4]{1,0:T(4,128)}) custom-call(bf16[128,1024]{1,0:T(8,128)(2,1)S(1)} %get-tuple-element.15.weight_ref, bf16[128,1024]{1,0:T(8,128)(2,1)S(1)} %half_product.1.half_ref.refs_0_, bf16[128,1024]{1,0:T(8,128)(2,1)S(1)} %collective-permute-done.10.refs_1_, ...), custom_call_target="tpu_custom_call" | custom-call | flops 268435456 | bytes 4194304 | tf_op jit(solution)/shard_map/dress/pallas_call | solution.py:194
  (15 shorter events, 0.1 us)
Async XLA Ops:
  2.4 18.9 %collective-permute-start.1 = (bf16[5,128,256]{2,1,0:T(8,128)(2,1)S(1)}, bf16[5,128,256]{2,1,0:T(8,128)(2,1)S(1)}, u32[]{:S(2)}, u32[]{:S(2)}) collective-permute-start(bf16[5,128,256]{2,1,0:T(8,128)(2,1)S(1)} %get-tuple-element.13.refs_0_), channel_id=1, source_target_pairs={{0,16},{8,24},{16,0},{24,8},{1,17},{9,25},{17,1},{25,9},{2,18},{10... | collective-permute-start | bytes 983048 | tf_op jit(solution)/shard_map/ppermute | solution.py:18
  6.5 15.0 %collective-permute-start = (bf16[5,128,256]{2,1,0:T(8,128)(2,1)S(1)}, bf16[5,128,256]{2,1,0:T(8,128)(2,1)S(1)}, u32[]{:S(2)}, u32[]{:S(2)}) collective-permute-start(bf16[5,128,256]{2,1,0:T(8,128)(2,1)S(1)} %get-tuple-element.13.refs_0_), channel_id=1, source_target_pairs={{0,8},{8,0},{16,24},{24,16},{1,9},{9,1},{17,25},{25,17},{2,10},{10... | collective-permute-start | bytes 983048 | tf_op jit(solution)/shard_map/ppermute | solution.py:18
  8.1 14.9 %collective-permute-start.8 = (bf16[5,128,256]{2,1,0:T(8,128)(2,1)S(1)}, bf16[5,128,256]{2,1,0:T(8,128)(2,1)S(1)}, u32[]{:S(2)}, u32[]{:S(2)}) collective-permute-start(bf16[5,128,256]{2,1,0:T(8,128)(2,1)S(1)} %get-tuple-element.14.refs_4_), channel_id=1, source_target_pairs={{0,6},{1,7},{2,4},{3,5},{4,2},{5,3},{6,0},{7,1},{8,14},{9,15},{10,... | collective-permute-start | bytes 983048 | tf_op jit(solution)/shard_map/ppermute | solution.py:18
  10.5 14.5 %collective-permute-start.6 = (bf16[5,128,256]{2,1,0:T(8,128)(2,1)S(1)}, bf16[5,128,256]{2,1,0:T(8,128)(2,1)S(1)}, u32[]{:S(2)}, u32[]{:S(2)}) collective-permute-start(bf16[5,128,256]{2,1,0:T(8,128)(2,1)S(1)} %get-tuple-element.14.refs_4_), channel_id=1, source_target_pairs={{0,4},{1,5},{2,6},{3,7},{4,0},{5,1},{6,2},{7,3},{8,12},{9,13},{10,... | collective-permute-start | bytes 983048 | tf_op jit(solution)/shard_map/ppermute | solution.py:18
  11.0 13.9 %collective-permute-start.4 = (bf16[5,128,256]{2,1,0:T(8,128)(2,1)S(1)}, bf16[5,128,256]{2,1,0:T(8,128)(2,1)S(1)}, u32[]{:S(2)}, u32[]{:S(2)}) collective-permute-start(bf16[5,128,256]{2,1,0:T(8,128)(2,1)S(1)} %get-tuple-element.14.refs_4_), channel_id=1, source_target_pairs={{0,2},{1,3},{2,0},{3,1},{4,6},{5,7},{6,4},{7,5},{8,10},{9,11},{10,... | collective-permute-start | bytes 983048 | tf_op jit(solution)/shard_map/ppermute | solution.py:18
  21.3 4.2 %collective-permute-start.3 = (bf16[5,128,256]{2,1,0:T(8,128)(2,1)S(1)}, bf16[5,128,256]{2,1,0:T(8,128)(2,1)S(1)}, u32[]{:S(2)}, u32[]{:S(2)}) collective-permute-start(bf16[5,128,256]{2,1,0:T(8,128)(2,1)S(1)} %get-tuple-element.14.refs_4_), channel_id=1, source_target_pairs={{0,1},{1,0},{2,3},{3,2},{4,5},{5,4},{6,7},{7,6},{8,9},{9,8},{10,11... | collective-permute-start | bytes 983048 | tf_op jit(solution)/shard_map/ppermute | solution.py:18
  21.5 9.9 %collective-permute-start.2 = (bf16[5,128,256]{2,1,0:T(8,128)(2,1)S(1)}, bf16[5,128,256]{2,1,0:T(8,128)(2,1)S(1)}, u32[]{:S(2)}, u32[]{:S(2)}) collective-permute-start(bf16[5,128,256]{2,1,0:T(8,128)(2,1)S(1)} %collective-permute-done.1.refs_2_), channel_id=1, source_target_pairs={{0,8},{8,0},{16,24},{24,16},{1,9},{9,1},{17,25},{25,17},{2,10},{10... | collective-permute-start | bytes 983048 | tf_op jit(solution)/shard_map/ppermute | solution.py:18
  23.0 8.5 %collective-permute-start.9 = (bf16[5,128,256]{2,1,0:T(8,128)(2,1)S(1)}, bf16[5,128,256]{2,1,0:T(8,128)(2,1)S(1)}, u32[]{:S(2)}, u32[]{:S(2)}) collective-permute-start(bf16[5,128,256]{2,1,0:T(8,128)(2,1)S(1)} %collective-permute-done.8.refs_10_), channel_id=1, source_target_pairs={{0,1},{1,0},{2,3},{3,2},{4,5},{5,4},{6,7},{7,6},{8,9},{9,8},{10,11... | collective-permute-start | bytes 983048 | tf_op jit(solution)/shard_map/ppermute | solution.py:18
  25.0 6.5 %collective-permute-start.7 = (bf16[5,128,256]{2,1,0:T(8,128)(2,1)S(1)}, bf16[5,128,256]{2,1,0:T(8,128)(2,1)S(1)}, u32[]{:S(2)}, u32[]{:S(2)}) collective-permute-start(bf16[5,128,256]{2,1,0:T(8,128)(2,1)S(1)} %collective-permute-done.6.refs_8_), channel_id=1, source_target_pairs={{0,1},{1,0},{2,3},{3,2},{4,5},{5,4},{6,7},{7,6},{8,9},{9,8},{10,11... | collective-permute-start | bytes 983048 | tf_op jit(solution)/shard_map/ppermute | solution.py:18
  25.0 6.5 %collective-permute-start.5 = (bf16[5,128,256]{2,1,0:T(8,128)(2,1)S(1)}, bf16[5,128,256]{2,1,0:T(8,128)(2,1)S(1)}, u32[]{:S(2)}, u32[]{:S(2)}) collective-permute-start(bf16[5,128,256]{2,1,0:T(8,128)(2,1)S(1)} %collective-permute-done.4.refs_6_), channel_id=1, source_target_pairs={{0,1},{1,0},{2,3},{3,2},{4,5},{5,4},{6,7},{7,6},{8,9},{9,8},{10,11... | collective-permute-start | bytes 983048 | tf_op jit(solution)/shard_map/ppermute | solution.py:18
  32.0 17.2 %collective-permute-start.13 = (bf16[128,1024]{1,0:T(8,128)(2,1)S(1)}, bf16[128,1024]{1,0:T(8,128)(2,1)S(1)}, u32[]{:S(2)}, u32[]{:S(2)}) collective-permute-start(bf16[128,1024]{1,0:T(8,128)(2,1)S(1)} %half_product.1.half_ref.refs_0_), channel_id=1, source_target_pairs={{0,6},{1,7},{2,4},{3,5},{4,2},{5,3},{6,0},{7,1},{8,14},{9,15},{10,... | collective-permute-start | bytes 786440 | tf_op jit(solution)/shard_map/ppermute | solution.py:18
  34.5 14.6 %collective-permute-start.12 = (bf16[128,1024]{1,0:T(8,128)(2,1)S(1)}, bf16[128,1024]{1,0:T(8,128)(2,1)S(1)}, u32[]{:S(2)}, u32[]{:S(2)}) collective-permute-start(bf16[128,1024]{1,0:T(8,128)(2,1)S(1)} %half_product.1.half_ref.refs_0_), channel_id=1, source_target_pairs={{0,4},{1,5},{2,6},{3,7},{4,0},{5,1},{6,2},{7,3},{8,12},{9,13},{10,... | collective-permute-start | bytes 786440 | tf_op jit(solution)/shard_map/ppermute | solution.py:18
  35.1 14.1 %collective-permute-start.11 = (bf16[128,1024]{1,0:T(8,128)(2,1)S(1)}, bf16[128,1024]{1,0:T(8,128)(2,1)S(1)}, u32[]{:S(2)}, u32[]{:S(2)}) collective-permute-start(bf16[128,1024]{1,0:T(8,128)(2,1)S(1)} %half_product.1.half_ref.refs_0_), channel_id=1, source_target_pairs={{0,2},{1,3},{2,0},{3,1},{4,6},{5,7},{6,4},{7,5},{8,10},{9,11},{10,... | collective-permute-start | bytes 786440 | tf_op jit(solution)/shard_map/ppermute | solution.py:18
  35.5 13.6 %collective-permute-start.10 = (bf16[128,1024]{1,0:T(8,128)(2,1)S(1)}, bf16[128,1024]{1,0:T(8,128)(2,1)S(1)}, u32[]{:S(2)}, u32[]{:S(2)}) collective-permute-start(bf16[128,1024]{1,0:T(8,128)(2,1)S(1)} %half_product.1.half_ref.refs_0_), channel_id=1, source_target_pairs={{0,1},{1,0},{2,3},{3,2},{4,5},{5,4},{6,7},{7,6},{8,9},{9,8},{10,11... | collective-permute-start | bytes 786440 | tf_op jit(solution)/shard_map/ppermute | solution.py:18
  49.2 1.6 %collective-permute-start.14 = (bf16[128,1024]{1,0:T(8,128)(2,1)S(1)}, bf16[128,1024]{1,0:T(8,128)(2,1)S(1)}, u32[]{:S(2)}, u32[]{:S(2)}) collective-permute-start(bf16[128,1024]{1,0:T(8,128)(2,1)S(1)} %collective-permute-done.11.refs_2_), channel_id=1, source_target_pairs={{0,1},{1,0},{2,3},{3,2},{4,5},{5,4},{6,7},{7,6},{8,9},{9,8},{10,11... | collective-permute-start | bytes 786440 | tf_op jit(solution)/shard_map/ppermute | solution.py:18
  49.2 1.9 %collective-permute-start.15 = (bf16[128,1024]{1,0:T(8,128)(2,1)S(1)}, bf16[128,1024]{1,0:T(8,128)(2,1)S(1)}, u32[]{:S(2)}, u32[]{:S(2)}) collective-permute-start(bf16[128,1024]{1,0:T(8,128)(2,1)S(1)} %collective-permute-done.12.refs_4_), channel_id=1, source_target_pairs={{0,1},{1,0},{2,3},{3,2},{4,5},{5,4},{6,7},{7,6},{8,9},{9,8},{10,11... | collective-permute-start | bytes 786440 | tf_op jit(solution)/shard_map/ppermute | solution.py:18
  49.7 1.8 %collective-permute-start.16 = (bf16[128,1024]{1,0:T(8,128)(2,1)S(1)}, bf16[128,1024]{1,0:T(8,128)(2,1)S(1)}, u32[]{:S(2)}, u32[]{:S(2)}) collective-permute-start(bf16[128,1024]{1,0:T(8,128)(2,1)S(1)} %collective-permute-done.13.refs_6_), channel_id=1, source_target_pairs={{0,1},{1,0},{2,3},{3,2},{4,5},{5,4},{6,7},{7,6},{8,9},{9,8},{10,11... | collective-permute-start | bytes 786440 | tf_op jit(solution)/shard_map/ppermute | solution.py:18

commit v2 on v1

--- a/solution.py
+++ b/solution.py
@@ -168,67 +168,95 @@
     )(half_block, *weights, *bundles)
 
 
-def dress_kernel(n_plane, total_ao, weight_ref, *refs):
-    halves, (shares_ref, out_ref, polar_ref) = refs[:n_plane], refs[n_plane:]
-    mu, aux, nu = out_ref.shape
+def near_kernel(places, total_ao, weight_ref, shares_ref, *refs):
+    halves, (part_ref, polar_ref) = refs[:-2], refs[-2:]
+    aux, mu, nu = part_ref.shape
     plane = plane_index()
-    sums = []
     for q in range(aux):
         total = jnp.zeros((mu, nu), jnp.float32)
-        for k in range(n_plane):
+        for k, ref in zip(places, halves):
             total += jnp.dot(
                 weight_ref[:, pl.ds(pl.multiple_of((plane ^ k) * mu, mu), mu)],
-                halves[k][:, q * nu : (q + 1) * nu],
+                ref[:, q * nu : (q + 1) * nu],
                 preferred_element_type=jnp.float32,
             )
-        sums.append(total)
-    out_ref[...] = jnp.stack(sums, axis=1).astype(out_ref.dtype)
+        part_ref[q] = total
     polar = jnp.sum(shares_ref[...], axis=0) / total_ao
     for p in range(aux):
         polar_ref[p : p + 1, :] = polar[:, p * aux : (p + 1) * aux]
 
 
-def dress(weight, halves, shares, aux, total_ao):
+def near(weight, halves, shares, aux, total_ao):
     mu, width = halves[0].shape
-    n_plane = len(halves)
-    return pl.pallas_call(
-        functools.partial(dress_kernel, n_plane, total_ao),
+    return pl.pallas_call(
+        functools.partial(near_kernel, list(halves), total_ao),
         out_shape=(
-            jax.ShapeDtypeStruct((mu, aux, width // aux), weight.dtype),
+            jax.ShapeDtypeStruct((aux, mu, width // aux), jnp.float32),
             jax.ShapeDtypeStruct((aux, aux), jnp.float32),
         ),
-        in_specs=[VMEM] * (n_plane + 2),
+        in_specs=[VMEM] * (2 + len(halves)),
         out_specs=(VMEM, VMEM),
         compiler_params=pltpu.CompilerParams(vmem_limit_bytes=ROOM),
         cost_estimate=pl.CostEstimate(
-            flops=2 * mu * mu * width * n_plane, bytes_accessed=4 * n_plane * mu * width, transcendentals=0
+            flops=2 * mu * mu * width * len(halves), bytes_accessed=4 * len(halves) * mu * width, transcendentals=0
+        ),
+        name="near",
+    )(weight, shares, *halves.values())
+
+
+def dress_kernel(places, weight_ref, part_ref, *refs):
+    halves, out_ref = refs[:-1], refs[-1]
+    mu, aux, nu = out_ref.shape
+    plane = plane_index()
+    for q in range(aux):
+        total = part_ref[q]
+        for k, ref in zip(places, halves):
+            total += jnp.dot(
+                weight_ref[:, pl.ds(pl.multiple_of((plane ^ k) * mu, mu), mu)],
+                ref[:, q * nu : (q + 1) * nu],
+                preferred_element_type=jnp.float32,
+            )
+        out_ref[:, q, :] = total.astype(out_ref.dtype)
+
+
+def dress(weight, part, halves):
+    aux, mu, nu = part.shape
+    return pl.pallas_call(
+        functools.partial(dress_kernel, list(halves)),
+        out_shape=jax.ShapeDtypeStruct((mu, aux, nu), weight.dtype),
+        in_specs=[VMEM] * (2 + len(halves)),
+        out_specs=VMEM,
+        compiler_params=pltpu.CompilerParams(vmem_limit_bytes=ROOM),
+        cost_estimate=pl.CostEstimate(
+            flops=2 * aux * mu * mu * nu * len(halves),
+            bytes_accessed=4 * len(halves) * aux * mu * nu,
+            transcendentals=0,
         ),
         name="dress",
-    )(weight, *halves, shares)
+    )(weight, part, *halves.values())
 
 
 def on_device(tensor_tiles, tile_pairs, tile_counts, occupied, virtual):
     aux = tensor_tiles.shape[1]
     nu = virtual.shape[1]
     n_row, n_plane = lax.axis_size("row"), lax.axis_size("col") * lax.axis_size("rep")
-    near = list(range(2, n_plane, 2))
+    near_chips = list(range(2, n_plane, 2))
     sibling = lambda value: flip(value, PLANE, 1, n_plane)
 
     line, bundle = place(tile_pairs, tile_counts, tensor_tiles, occupied, virtual)
     lines = gather_row(line, n_row)
     bundles = []
-    for value in [bundle] + [flip(bundle, PLANE, k, n_plane) for k in near]:
+    for value in [bundle] + [flip(bundle, PLANE, k, n_plane) for k in near_chips]:
         bundles += [value, sibling(value)]
     own = half(lines, bundles)
 
-    arrivals = [flip(own, PLANE, k, n_plane) for k in near]
+    arrivals = [flip(own, PLANE, k, n_plane) for k in near_chips]
     other = sibling(own)
     weight, share = share_of(own, lines, bundles)
     shares, (other, arrivals) = after(lax.all_to_all(share, EVERY, 0, 0), (other, arrivals))
-    halves = [own, other]
-    for value in arrivals:
-        halves += [value, sibling(value)]
-    dressed, polar = dress(weight, halves, shares, aux, n_row * nu)
+    here = {0: own, 1: other, **dict(zip(near_chips, arrivals))}
+    part, polar = near(weight, here, shares, aux, n_row * nu)
+    dressed = dress(weight, part, {k ^ 1: sibling(here[k]) for k in near_chips})
     return polar, dressed
 
 

time: 53.5 us -> 53 us (level)
  waiting for transfers between devices: 19.6 us -> 18.6 us
  Pallas kernels: 4.24 us -> 4.79 us
    ppermute x17, waiting for transfers between devices: 19.6 us -> 18.6 us  [flip(): return lax.ppermute(value, axes, [(i, i ^ mask) for i in range(count)])]
    pallas_call x1 -> x2, Pallas kernels: 1.79 us -> 2.33 us  [the longest x1 1.33 us: dress(): pl.pallas_call(functools.partial(dress_kernel, list(halves)), out_shape=j...]
  transfers between devices with their start and end apart: 17 -> 17, of which waited for: 7 -> 6; matrix products, arithmetic and copies ran while one was open for 0% -> 0% of each run, Pallas kernels for 2% -> 4%
where the time goes in v2:
time: 53 us; the launch traced here: 52.9 us
  waiting for transfers between devices  18.6 us (35%)
  starting transfers between devices  15.4 us (29%)
  blocking collectives  12.7 us (24%)
  Pallas kernels  4.79 us (9%)
  between operations  1.34 us (3%)
    ppermute x17, waiting for transfers between devices, flip(): return lax.ppermute(value, axes, [(i, i ^ mask) for i in range(count)])  18.6 us
    ppermute x17, starting transfers between devices, flip(): return lax.ppermute(value, axes, [(i, i ^ mask) for i in range(count)])  15.4 us
    all_to_all x1, blocking collectives, on_device(): lax.all_to_all(share, EVERY, 0, 0)  12.7 us
    pallas_call x1, Pallas kernels, dress(): pl.pallas_call(functools.partial(dress_kernel, list(halves)), out_shape=j...  1.33 us
    pallas_call x1, Pallas kernels, place(): pl.pallas_call(functools.partial(place_kernel, nu // tile), out_shape=(sh...  1.11 us
  transfers between devices with their start and end apart: 17, of which 6 were waited for; matrix products, arithmetic and copies ran while one was open for 0% of the time, Pallas kernels for 4%

profile of v2, /device:TPU:0, one launch (start us, length us, event | category | flops | bytes accessed | tf_op | source)
XLA Modules:
  0.0 52.9 jit_solution(4611819962939317495)
XLA Ops:
  1.3 1.1 %place.1 = (bf16[5,128,256]{2,1,0:T(8,128)(2,1)S(1)}, bf16[5,128,256]{2,1,0:T(8,128)(2,1)S(1)}) custom-call(s32[1]{0:T(128)S(6)} %copy.7.counts_ref, s32[2]{0:T(128)} %pairs_any.1, bf16[2,4,128,128]{3,2,1,0:T(8,128)(2,1)} %tiles_any.1, bf16[128,256]{1,0:T(8,128)(2,1)} %weight_any.1, bf16[128,256]{1,0:T(8,128)(2,1)} %column_any.1), custom_call_target="tpu_custom_call" | custom-call | bytes 786432 | tf_op jit(solution)/shard_map/place/pallas_call | solution.py:77
  2.4 4.1 %collective-permute-start.1 = (bf16[5,128,256]{2,1,0:T(8,128)(2,1)S(1)}, bf16[5,128,256]{2,1,0:T(8,128)(2,1)S(1)}, u32[]{:S(2)}, u32[]{:S(2)}) collective-permute-start(bf16[5,128,256]{2,1,0:T(8,128)(2,1)S(1)} %get-tuple-element.13.refs_0_), channel_id=1, source_target_pairs={{0,16},{8,24},{16,0},{24,8},{1,17},{9,25},{17,1},{25,9},{2,18},{10... | collective-permute-start | bytes 983048 | tf_op jit(solution)/shard_map/ppermute | solution.py:18
  6.5 1.6 %collective-permute-start = (bf16[5,128,256]{2,1,0:T(8,128)(2,1)S(1)}, bf16[5,128,256]{2,1,0:T(8,128)(2,1)S(1)}, u32[]{:S(2)}, u32[]{:S(2)}) collective-permute-start(bf16[5,128,256]{2,1,0:T(8,128)(2,1)S(1)} %get-tuple-element.13.refs_0_), channel_id=1, source_target_pairs={{0,8},{8,0},{16,24},{24,16},{1,9},{9,1},{17,25},{25,17},{2,10},{10... | collective-permute-start | bytes 983048 | tf_op jit(solution)/shard_map/ppermute | solution.py:18
  8.1 2.4 %collective-permute-start.8 = (bf16[5,128,256]{2,1,0:T(8,128)(2,1)S(1)}, bf16[5,128,256]{2,1,0:T(8,128)(2,1)S(1)}, u32[]{:S(2)}, u32[]{:S(2)}) collective-permute-start(bf16[5,128,256]{2,1,0:T(8,128)(2,1)S(1)} %get-tuple-element.14.refs_4_), channel_id=1, source_target_pairs={{0,6},{1,7},{2,4},{3,5},{4,2},{5,3},{6,0},{7,1},{8,14},{9,15},{10,... | collective-permute-start | bytes 983048 | tf_op jit(solution)/shard_map/ppermute | solution.py:18
  10.5 0.5 %collective-permute-start.6 = (bf16[5,128,256]{2,1,0:T(8,128)(2,1)S(1)}, bf16[5,128,256]{2,1,0:T(8,128)(2,1)S(1)}, u32[]{:S(2)}, u32[]{:S(2)}) collective-permute-start(bf16[5,128,256]{2,1,0:T(8,128)(2,1)S(1)} %get-tuple-element.14.refs_4_), channel_id=1, source_target_pairs={{0,4},{1,5},{2,6},{3,7},{4,0},{5,1},{6,2},{7,3},{8,12},{9,13},{10,... | collective-permute-start | bytes 983048 | tf_op jit(solution)/shard_map/ppermute | solution.py:18
  11.0 0.5 collective-permute-start.4
  11.6 9.8 %collective-permute-done.1.refs_2_ = bf16[5,128,256]{2,1,0:T(8,128)(2,1)S(1)} collective-permute-done((bf16[5,128,256]{2,1,0:T(8,128)(2,1)S(1)}, bf16[5,128,256]{2,1,0:T(8,128)(2,1)S(1)}, u32[]{:S(2)}, u32[]{:S(2)}) %collective-permute-start.1) | collective-permute-done | bytes 327712 | tf_op jit(solution)/shard_map/ppermute | solution.py:18
  21.3 0.2 collective-permute-done.refs_1_
  21.5 1.5 %collective-permute-start.2 = (bf16[5,128,256]{2,1,0:T(8,128)(2,1)S(1)}, bf16[5,128,256]{2,1,0:T(8,128)(2,1)S(1)}, u32[]{:S(2)}, u32[]{:S(2)}) collective-permute-start(bf16[5,128,256]{2,1,0:T(8,128)(2,1)S(1)} %collective-permute-done.1.refs_2_), channel_id=1, source_target_pairs={{0,8},{8,0},{16,24},{24,16},{1,9},{9,1},{17,25},{25,17},{2,10},{10... | collective-permute-start | bytes 983048 | tf_op jit(solution)/shard_map/ppermute | solution.py:18
  23.0 2.0 %collective-permute-done.6.refs_8_ = bf16[5,128,256]{2,1,0:T(8,128)(2,1)S(1)} collective-permute-done((bf16[5,128,256]{2,1,0:T(8,128)(2,1)S(1)}, bf16[5,128,256]{2,1,0:T(8,128)(2,1)S(1)}, u32[]{:S(2)}, u32[]{:S(2)}) %collective-permute-start.6) | collective-permute-done | bytes 327712 | tf_op jit(solution)/shard_map/ppermute | solution.py:18
  25.0 0.5 collective-permute-start.5
  25.5 6.0 %collective-permute-done.2.refs_3_ = bf16[5,128,256]{2,1,0:T(8,128)(2,1)S(1)} collective-permute-done((bf16[5,128,256]{2,1,0:T(8,128)(2,1)S(1)}, bf16[5,128,256]{2,1,0:T(8,128)(2,1)S(1)}, u32[]{:S(2)}, u32[]{:S(2)}) %collective-permute-start.2) | collective-permute-done | bytes 327712 | tf_op jit(solution)/shard_map/ppermute | solution.py:18
  31.5 0.5 half_product.1.half_ref.refs_0_
  32.0 2.6 %collective-permute-start.13 = (bf16[128,1024]{1,0:T(8,128)(2,1)S(1)}, bf16[128,1024]{1,0:T(8,128)(2,1)S(1)}, u32[]{:S(2)}, u32[]{:S(2)}) collective-permute-start(bf16[128,1024]{1,0:T(8,128)(2,1)S(1)} %half_product.1.half_ref.refs_0_), channel_id=1, source_target_pairs={{0,6},{1,7},{2,4},{3,5},{4,2},{5,3},{6,0},{7,1},{8,14},{9,15},{10,... | collective-permute-start | bytes 786440 | tf_op jit(solution)/shard_map/ppermute | solution.py:18
  34.5 0.5 %collective-permute-start.12 = (bf16[128,1024]{1,0:T(8,128)(2,1)S(1)}, bf16[128,1024]{1,0:T(8,128)(2,1)S(1)}, u32[]{:S(2)}, u32[]{:S(2)}) collective-permute-start(bf16[128,1024]{1,0:T(8,128)(2,1)S(1)} %half_product.1.half_ref.refs_0_), channel_id=1, source_target_pairs={{0,4},{1,5},{2,6},{3,7},{4,0},{5,1},{6,2},{7,3},{8,12},{9,13},{10,... | collective-permute-start | bytes 786440 | tf_op jit(solution)/shard_map/ppermute | solution.py:18
  35.1 0.5 collective-permute-start.11
  35.5 0.9 %polar_share.1 = (bf16[128,1024]{1,0:T(8,128)(2,1)S(1)}, f32[32,1,128]{2,1,0:T(1,128)S(1)}) custom-call(bf16[128,1024]{1,0:T(8,128)(2,1)S(1)} %half_product.1.half_ref.refs_0_, bf16[5,128,256]{2,1,0:T(8,128)(2,1)S(1)} %get-tuple-element.13.refs_0_, bf16[5,128,256]{2,1,0:T(8,128)(2,1)S(1)} %collective-permute-done.refs_1_, ...), custom_call_target="tpu_custom_call" | custom-call | flops 268435456 | bytes 4194304 | tf_op jit(solution)/shard_map/polar_share/pallas_call | solution.py:155
  36.4 12.7 %all_to_all.5.shares_ref = f32[32,1,128]{2,1,0:T(1,128)S(1)} all-to-all(f32[32,1,128]{2,1,0:T(1,128)S(1)} %get-tuple-element.16), channel_id=1, replica_groups=mesh['row'=4,'col'=2,'rep'=4] {'row','col','rep'}, dimensions={0} | all-to-all | bytes 32768 | tf_op jit(solution)/shard_map/all_to_all | solution.py:256
  49.2 0.5 collective-permute-start.15
  49.7 0.1 collective-permute-start.16
  49.8 1.0 %near.1 = (f32[4,128,256]{2,1,0:T(8,128)S(1)}, f32[4,4]{1,0:T(4,128)}) custom-call(bf16[128,1024]{1,0:T(8,128)(2,1)S(1)} %get-tuple-element.15.weight_ref, f32[32,1,128]{2,1,0:T(1,128)S(1)} %all_to_all.5.shares_ref, bf16[128,1024]{1,0:T(8,128)(2,1)S(1)} %half_product.1.half_ref.refs_0_, bf16[128,1024]{1,0:T(8,128)(2,1)S(1)} %collective-permute-done.10.refs_1_, ...), custom_call_target="tpu_custom_call" | custom-call | flops 167772160 | bytes 2621440 | tf_op jit(solution)/shard_map/near/pallas_call | solution.py:191
  50.8 0.3 collective-permute-done.15.refs_1_
  51.1 0.4 collective-permute-done.16.refs_2_
  51.5 1.3 %dress.1 = bf16[128,4,256]{2,1,0:T(4,128)(2,1)} custom-call(bf16[128,1024]{1,0:T(8,128)(2,1)S(1)} %get-tuple-element.15.weight_ref, f32[4,128,256]{2,1,0:T(8,128)S(1)} %get-tuple-element.23.part_ref, bf16[128,1024]{1,0:T(8,128)(2,1)S(1)} %collective-permute-done.14.refs_0_, bf16[128,1024]{1,0:T(8,128)(2,1)S(1)} %collective-permute-done.15.refs_1_, ...), custom_call_target="tpu_custom_call" | custom-call | flops 100663296 | bytes 1572864 | tf_op jit(solution)/shard_map/dress/pallas_call | solution.py:224
  (16 shorter events, 0.1 us)
Async XLA Ops:
  2.4 18.9 %collective-permute-start.1 = (bf16[5,128,256]{2,1,0:T(8,128)(2,1)S(1)}, bf16[5,128,256]{2,1,0:T(8,128)(2,1)S(1)}, u32[]{:S(2)}, u32[]{:S(2)}) collective-permute-start(bf16[5,128,256]{2,1,0:T(8,128)(2,1)S(1)} %get-tuple-element.13.refs_0_), channel_id=1, source_target_pairs={{0,16},{8,24},{16,0},{24,8},{1,17},{9,25},{17,1},{25,9},{2,18},{10... | collective-permute-start | bytes 983048 | tf_op jit(solution)/shard_map/ppermute | solution.py:18
  6.5 15.0 %collective-permute-start = (bf16[5,128,256]{2,1,0:T(8,128)(2,1)S(1)}, bf16[5,128,256]{2,1,0:T(8,128)(2,1)S(1)}, u32[]{:S(2)}, u32[]{:S(2)}) collective-permute-start(bf16[5,128,256]{2,1,0:T(8,128)(2,1)S(1)} %get-tuple-element.13.refs_0_), channel_id=1, source_target_pairs={{0,8},{8,0},{16,24},{24,16},{1,9},{9,1},{17,25},{25,17},{2,10},{10... | collective-permute-start | bytes 983048 | tf_op jit(solution)/shard_map/ppermute | solution.py:18
  8.1 14.9 %collective-permute-start.8 = (bf16[5,128,256]{2,1,0:T(8,128)(2,1)S(1)}, bf16[5,128,256]{2,1,0:T(8,128)(2,1)S(1)}, u32[]{:S(2)}, u32[]{:S(2)}) collective-permute-start(bf16[5,128,256]{2,1,0:T(8,128)(2,1)S(1)} %get-tuple-element.14.refs_4_), channel_id=1, source_target_pairs={{0,6},{1,7},{2,4},{3,5},{4,2},{5,3},{6,0},{7,1},{8,14},{9,15},{10,... | collective-permute-start | bytes 983048 | tf_op jit(solution)/shard_map/ppermute | solution.py:18
  10.5 14.5 %collective-permute-start.6 = (bf16[5,128,256]{2,1,0:T(8,128)(2,1)S(1)}, bf16[5,128,256]{2,1,0:T(8,128)(2,1)S(1)}, u32[]{:S(2)}, u32[]{:S(2)}) collective-permute-start(bf16[5,128,256]{2,1,0:T(8,128)(2,1)S(1)} %get-tuple-element.14.refs_4_), channel_id=1, source_target_pairs={{0,4},{1,5},{2,6},{3,7},{4,0},{5,1},{6,2},{7,3},{8,12},{9,13},{10,... | collective-permute-start | bytes 983048 | tf_op jit(solution)/shard_map/ppermute | solution.py:18
  11.0 13.9 %collective-permute-start.4 = (bf16[5,128,256]{2,1,0:T(8,128)(2,1)S(1)}, bf16[5,128,256]{2,1,0:T(8,128)(2,1)S(1)}, u32[]{:S(2)}, u32[]{:S(2)}) collective-permute-start(bf16[5,128,256]{2,1,0:T(8,128)(2,1)S(1)} %get-tuple-element.14.refs_4_), channel_id=1, source_target_pairs={{0,2},{1,3},{2,0},{3,1},{4,6},{5,7},{6,4},{7,5},{8,10},{9,11},{10,... | collective-permute-start | bytes 983048 | tf_op jit(solution)/shard_map/ppermute | solution.py:18
  21.3 4.2 %collective-permute-start.3 = (bf16[5,128,256]{2,1,0:T(8,128)(2,1)S(1)}, bf16[5,128,256]{2,1,0:T(8,128)(2,1)S(1)}, u32[]{:S(2)}, u32[]{:S(2)}) collective-permute-start(bf16[5,128,256]{2,1,0:T(8,128)(2,1)S(1)} %get-tuple-element.14.refs_4_), channel_id=1, source_target_pairs={{0,1},{1,0},{2,3},{3,2},{4,5},{5,4},{6,7},{7,6},{8,9},{9,8},{10,11... | collective-permute-start | bytes 983048 | tf_op jit(solution)/shard_map/ppermute | solution.py:18
  21.5 9.9 %collective-permute-start.2 = (bf16[5,128,256]{2,1,0:T(8,128)(2,1)S(1)}, bf16[5,128,256]{2,1,0:T(8,128)(2,1)S(1)}, u32[]{:S(2)}, u32[]{:S(2)}) collective-permute-start(bf16[5,128,256]{2,1,0:T(8,128)(2,1)S(1)} %collective-permute-done.1.refs_2_), channel_id=1, source_target_pairs={{0,8},{8,0},{16,24},{24,16},{1,9},{9,1},{17,25},{25,17},{2,10},{10... | collective-permute-start | bytes 983048 | tf_op jit(solution)/shard_map/ppermute | solution.py:18
  23.0 8.5 %collective-permute-start.9 = (bf16[5,128,256]{2,1,0:T(8,128)(2,1)S(1)}, bf16[5,128,256]{2,1,0:T(8,128)(2,1)S(1)}, u32[]{:S(2)}, u32[]{:S(2)}) collective-permute-start(bf16[5,128,256]{2,1,0:T(8,128)(2,1)S(1)} %collective-permute-done.8.refs_10_), channel_id=1, source_target_pairs={{0,1},{1,0},{2,3},{3,2},{4,5},{5,4},{6,7},{7,6},{8,9},{9,8},{10,11... | collective-permute-start | bytes 983048 | tf_op jit(solution)/shard_map/ppermute | solution.py:18
  25.0 6.5 %collective-permute-start.7 = (bf16[5,128,256]{2,1,0:T(8,128)(2,1)S(1)}, bf16[5,128,256]{2,1,0:T(8,128)(2,1)S(1)}, u32[]{:S(2)}, u32[]{:S(2)}) collective-permute-start(bf16[5,128,256]{2,1,0:T(8,128)(2,1)S(1)} %collective-permute-done.6.refs_8_), channel_id=1, source_target_pairs={{0,1},{1,0},{2,3},{3,2},{4,5},{5,4},{6,7},{7,6},{8,9},{9,8},{10,11... | collective-permute-start | bytes 983048 | tf_op jit(solution)/shard_map/ppermute | solution.py:18
  25.0 6.5 %collective-permute-start.5 = (bf16[5,128,256]{2,1,0:T(8,128)(2,1)S(1)}, bf16[5,128,256]{2,1,0:T(8,128)(2,1)S(1)}, u32[]{:S(2)}, u32[]{:S(2)}) collective-permute-start(bf16[5,128,256]{2,1,0:T(8,128)(2,1)S(1)} %collective-permute-done.4.refs_6_), channel_id=1, source_target_pairs={{0,1},{1,0},{2,3},{3,2},{4,5},{5,4},{6,7},{7,6},{8,9},{9,8},{10,11... | collective-permute-start | bytes 983048 | tf_op jit(solution)/shard_map/ppermute | solution.py:18
  32.0 17.2 %collective-permute-start.13 = (bf16[128,1024]{1,0:T(8,128)(2,1)S(1)}, bf16[128,1024]{1,0:T(8,128)(2,1)S(1)}, u32[]{:S(2)}, u32[]{:S(2)}) collective-permute-start(bf16[128,1024]{1,0:T(8,128)(2,1)S(1)} %half_product.1.half_ref.refs_0_), channel_id=1, source_target_pairs={{0,6},{1,7},{2,4},{3,5},{4,2},{5,3},{6,0},{7,1},{8,14},{9,15},{10,... | collective-permute-start | bytes 786440 | tf_op jit(solution)/shard_map/ppermute | solution.py:18
  34.5 14.6 %collective-permute-start.12 = (bf16[128,1024]{1,0:T(8,128)(2,1)S(1)}, bf16[128,1024]{1,0:T(8,128)(2,1)S(1)}, u32[]{:S(2)}, u32[]{:S(2)}) collective-permute-start(bf16[128,1024]{1,0:T(8,128)(2,1)S(1)} %half_product.1.half_ref.refs_0_), channel_id=1, source_target_pairs={{0,4},{1,5},{2,6},{3,7},{4,0},{5,1},{6,2},{7,3},{8,12},{9,13},{10,... | collective-permute-start | bytes 786440 | tf_op jit(solution)/shard_map/ppermute | solution.py:18
  35.1 14.1 %collective-permute-start.11 = (bf16[128,1024]{1,0:T(8,128)(2,1)S(1)}, bf16[128,1024]{1,0:T(8,128)(2,1)S(1)}, u32[]{:S(2)}, u32[]{:S(2)}) collective-permute-start(bf16[128,1024]{1,0:T(8,128)(2,1)S(1)} %half_product.1.half_ref.refs_0_), channel_id=1, source_target_pairs={{0,2},{1,3},{2,0},{3,1},{4,6},{5,7},{6,4},{7,5},{8,10},{9,11},{10,... | collective-permute-start | bytes 786440 | tf_op jit(solution)/shard_map/ppermute | solution.py:18
  35.5 13.6 %collective-permute-start.10 = (bf16[128,1024]{1,0:T(8,128)(2,1)S(1)}, bf16[128,1024]{1,0:T(8,128)(2,1)S(1)}, u32[]{:S(2)}, u32[]{:S(2)}) collective-permute-start(bf16[128,1024]{1,0:T(8,128)(2,1)S(1)} %half_product.1.half_ref.refs_0_), channel_id=1, source_target_pairs={{0,1},{1,0},{2,3},{3,2},{4,5},{5,4},{6,7},{7,6},{8,9},{9,8},{10,11... | collective-permute-start | bytes 786440 | tf_op jit(solution)/shard_map/ppermute | solution.py:18
  49.2 1.7 %collective-permute-start.14 = (bf16[128,1024]{1,0:T(8,128)(2,1)S(1)}, bf16[128,1024]{1,0:T(8,128)(2,1)S(1)}, u32[]{:S(2)}, u32[]{:S(2)}) collective-permute-start(bf16[128,1024]{1,0:T(8,128)(2,1)S(1)} %collective-permute-done.11.refs_2_), channel_id=1, source_target_pairs={{0,1},{1,0},{2,3},{3,2},{4,5},{5,4},{6,7},{7,6},{8,9},{9,8},{10,11... | collective-permute-start | bytes 786440 | tf_op jit(solution)/shard_map/ppermute | solution.py:18
  49.2 1.9 %collective-permute-start.15 = (bf16[128,1024]{1,0:T(8,128)(2,1)S(1)}, bf16[128,1024]{1,0:T(8,128)(2,1)S(1)}, u32[]{:S(2)}, u32[]{:S(2)}) collective-permute-start(bf16[128,1024]{1,0:T(8,128)(2,1)S(1)} %collective-permute-done.12.refs_3_), channel_id=1, source_target_pairs={{0,1},{1,0},{2,3},{3,2},{4,5},{5,4},{6,7},{7,6},{8,9},{9,8},{10,11... | collective-permute-start | bytes 786440 | tf_op jit(solution)/shard_map/ppermute | solution.py:18
  49.7 1.8 %collective-permute-start.16 = (bf16[128,1024]{1,0:T(8,128)(2,1)S(1)}, bf16[128,1024]{1,0:T(8,128)(2,1)S(1)}, u32[]{:S(2)}, u32[]{:S(2)}) collective-permute-start(bf16[128,1024]{1,0:T(8,128)(2,1)S(1)} %collective-permute-done.13.refs_4_), channel_id=1, source_target_pairs={{0,1},{1,0},{2,3},{3,2},{4,5},{5,4},{6,7},{7,6},{8,9},{9,8},{10,11... | collective-permute-start | bytes 786440 | tf_op jit(solution)/shard_map/ppermute | solution.py:18
